TPU v7x, 128 devices: a whole 4x4x4 slice. The times are simulated.
128 devices in a mesh: frames: 16 (over z_lo, x, core), rows: 8 (over z_hi, y).
Axes of the slice: x: 4, y: 4, z: 4 (z_hi: 2, z_lo: 2; z = z_hi * 2 + z_lo), core: 2. Of those that a mesh axis runs over, the one named last changes fastest.
Arguments:
- video: bfloat16 [32, 64, 512, 256], P('frames', 'rows'), may hold values from -36 to 36
- w_time: bfloat16 [3, 256, 256], replicated, may hold values from -0.21875 to 0.21875
- w_proj: bfloat16 [256, 128], replicated, may hold values from -0.375 to 0.375
- w_space: bfloat16 [3, 3, 128, 128], replicated, may hold values from -0.1875 to 0.1875
- gn_gain: float32 [128], replicated, may hold values from 0.1 to 1.9
- gn_bias: float32 [128], replicated, may hold values from -3 to 3
- noise: bfloat16 [64, 64, 512, 128], P(None, 'rows', 'frames'), may hold values from -6 to 6
Outputs:
- sample: bfloat16 [64, 64, 512, 128], P(None, 'rows', 'frames')
All inputs are finite; a program needn't handle non-finite values.
Results may differ from a plain program's by a relative error of at most 0.0048.
The roundings to bfloat16 on the way count: a program that leaves them out, or rounds other values in their place, can miss the bound.
Values may be sent and summed in bfloat16 or wider, within the bound.
A program may use at most 192 MiB of HBM per device.

v0:
```python
import jax
import jax.numpy as jnp
from jax import lax
from jax.experimental import pallas as pl
from jax.experimental.pallas import tpu as pltpu
from jax.sharding import PartitionSpec as P

MESH = pl.DeviceIdType.MESH
NF, NR = 16, 8
GROUPS = 32
BF, F32 = jnp.bfloat16, jnp.float32

PEERS = [(dz, dx, dc) for dx in (2, 1, 3, 0) for dz in (1, 0) for dc in (0, 1) if (dz, dx, dc) != (0, 0, 0)]


def peer(f, k):
    dz, dx, dc = PEERS[k]
    z, x, c = f // 8, (f // 2) % 4, f % 2
    return ((z + dz) % 2) * 8 + ((x + dx) % 4) * 2 + (c + dc) % 2


def silu(v):
    h = 0.5 * v
    return h + h * jnp.tanh(h)


def gather_groups(parts):
    lane = lax.broadcasted_iota(jnp.int32, parts[0].shape, 1) & 3
    out = jnp.zeros(parts[0].shape, F32)
    for k, v in enumerate(parts):
        v = v + pltpu.roll(v, 127, 1)
        v = v + pltpu.roll(v, 126, 1)
        out = jnp.where(lane == k, pltpu.roll(v, k, 1) if k else v, out)
    return out


def spread_groups(v, k):
    lane = lax.broadcasted_iota(jnp.int32, v.shape, 1) & 3
    v = jnp.where(lane == k, v, 0.0)
    v = pltpu.roll(v, 128 - k, 1) if k else v
    v = v + pltpu.roll(v, 1, 1)
    return v + pltpu.roll(v, 2, 1)


def temporal(before, now, after, w3, wp):
    x = [v.reshape(512, 256) for v in (before, now, after)]
    taps = jnp.dot(jnp.concatenate(x, axis=1), w3[...], preferred_element_type=F32)
    mixed = (x[1].astype(F32) + silu(taps)).astype(BF)
    proj = jnp.dot(mixed, wp[...], preferred_element_type=F32).astype(BF)
    return proj.reshape(8, 2, 32, 128)


def border_keeps(f, r):
    return (jnp.where(r > 0, 1.0, 0.0), jnp.where(r < NR - 1, 1.0, 0.0),
            (jnp.where(f > 0, 1.0, 0.0), jnp.where(f < NF - 1, 1.0, 0.0)))


def norm_frame(now, nxt, line, place, pb, tb, ed, st, gain, bias, ea, ll, fld, keeps):
    keep_top, keep_bottom, keep_side = keeps
    line = pl.ds(line, 1)
    scale = st[1, line] * gain[...]
    shift = 0.5 * (bias[...] - st[0, line] * scale)
    scale = (0.5 if nxt is None else 0.25) * scale
    sub = lax.broadcasted_iota(jnp.int32, (8, 128), 0)

    def act_of(ref, before, after, keep=None):
        v = ref[before + now + after]
        if nxt is not None:
            v = v + ref[before + nxt + after]
        if keep is not None:
            keep[...] = v
        h = v.astype(F32) * scale + shift
        return h + h * jnp.tanh(h)

    for s in range(2):
        ea[s] = act_of(ed, (s,), ()) * keep_side[s]
    for R in range(10):
        E = 8 if R == 0 else R - 1 if R < 9 else 9
        el, er = ea[0, E:E + 1], ea[1, E:E + 1]
        if R == 0:
            a = act_of(tb, (0,), ()) * keep_top
            el, er = el * keep_top, er * keep_top
        elif R == 9:
            a = act_of(tb, (1,), ()) * keep_bottom
            el, er = el * keep_bottom, er * keep_bottom
        else:
            a = act_of(pb, (), (R - 1,), None if fld is None else fld.at[place, R - 1])
        tiles = [a[8 * i:8 * i + 8] for i in range(4)]
        down = [pltpu.roll(v, 1, 0) for v in tiles]
        up = [pltpu.roll(v, 7, 0) for v in tiles]
        left = [jnp.where(sub == 0, down[i - 1] if i else el, down[i]) for i in range(4)]
        right = [jnp.where(sub == 7, up[i + 1] if i < 3 else er, up[i]) for i in range(4)]
        for j, v in enumerate((jnp.concatenate(left, 0), a, jnp.concatenate(right, 0))):
            lane = 256 * j + 128 * (R % 2)
            ll[R // 2, 32 * place:32 * place + 32, lane:lane + 128] = v.astype(BF)


def fill_weights(ws, w0, w1):
    zero = jnp.zeros((128, 128), BF)
    for j in range(3):
        for a in range(2):
            for b in range(2):
                i = a - b
                at = (slice(256 * j + 128 * a, 256 * j + 128 * a + 128), slice(128 * b, 128 * b + 128))
                w0[at] = ws[i, j] if 0 <= i else zero
                i = 2 + a - b
                w1[at] = ws[i, j] if i <= 2 else zero


def conv_rows(count, ll, w0, w1):
    m = 32 * count
    sides = jnp.concatenate([ll[0:4].reshape(4 * m, 768), ll[1:5].reshape(4 * m, 768)], axis=1)
    res = jnp.dot(sides, jnp.concatenate([w0[...], w1[...]], axis=0), preferred_element_type=F32)
    return [res[m * (R // 2):m * (R // 2) + m, 128 * (R % 2):128 * (R % 2) + 128].reshape(count, 32, 128)
            for R in range(8)]


def conv_kernel(pb, tb, ed, st, early, ws, gain, bias, noise, out, w0, w1, ll_a, ll_b, fld_a, fld_b, ea):
    f, r = lax.axis_index("frames"), lax.axis_index("rows")
    g = pl.program_id(0)
    steps = pl.num_programs(0) - 1
    keeps = border_keeps(f, r)

    @pl.when(g == 0)
    def _():
        fill_weights(ws, w0, w1)

    def step(new, old):
        if new is not None:
            ll, fld = new
            for i, (_, at, nxt) in enumerate(LATE):
                norm_frame(slot_of(g, at), nxt and slot_of(g, nxt), L_ROWS * g + i, i,
                           pb, tb, ed, st, gain, bias, ea.at[i], ll, fld, keeps)
        if old is not None:
            ll, fld = old
            rows = conv_rows(len(LATE), ll, w0, w1)
            for R in range(8):
                for i, (k, _, nxt) in enumerate(LATE):
                    v = fld[i, R].astype(F32) * (1.0 if nxt is None else 0.5)
                    out[k, R] = (rows[R][i] + v + 0.3 * noise[k, R].astype(F32)).astype(BF)
            for i, (k, _, _) in enumerate(EARLY):
                out[k] = early[0, i]

    a, b = (ll_a, fld_a), (ll_b, fld_b)

    @pl.when(g == 0)
    def _():
        step(a, None)

    @pl.when((g > 0) & (g < steps) & (g % 2 == 0))
    def _():
        step(a, b)

    @pl.when((g < steps) & (g % 2 == 1))
    def _():
        step(b, a)

    @pl.when(g == steps)
    def _():
        step(None, b)


EARLY = ((2, (0, 2), None), (3, (0, 2), (0, 3)), (4, (0, 3), None))
LATE = ((0, (0, 1), None), (1, (0, 1), (0, 2)), (5, (0, 3), (1, 0)), (6, (1, 0), None), (7, (1, 0), (1, 1)))
HALO_AT = ((0, 1), (2, 3))
E_ROWS, L_ROWS = 4, 6


def slot_of(q, at):
    if at == (1, 1):
        return q + 1, jnp.where(q == 7, 0, 1)
    return q + at[0], at[1]


def move_kernel(
    video, wt, wp, ws, gain, bias, noise, pb_out, tb_out, ed_out, st_out, early_out,
    vv, inner, halo, relay, w3, si, so, pb, tb, eo, ed,
    st_e, s1e, r1e, s2e, r2e, stat_e, st_l, s1l, r1l, s2l, r2l,
    nz, w0, w1, ll, ea, res_e,
    lsem, ns, nr, hs, hr, ls, lr, is_, ir, os, or_, ts, tr, es, er, sem_e1, sem_e2, sem_l1, sem_l2, osem,
):
    f, r = lax.axis_index("frames"), lax.axis_index("rows")
    z, x, c = f // 8, (f // 2) % 4, f % 2
    chip = f // 2
    sgn = 2 * c - 1
    is_end = (f == 0) | (f == NF - 1)
    not_end = jnp.logical_not(is_end)
    outer_frame, inner_frame = c, 1 - c
    outer_dev = jnp.clip(f + sgn, 0, NF - 1)
    inner_dev = f + 1 - 2 * c

    def wait_in(ref, sem):
        pltpu.make_async_copy(ref, ref, sem).wait()

    def column(zz, xx):
        return pl.ds(pl.multiple_of(zz * 256 + xx * 64, 64), 64)

    def far_first(i):
        j = i // 2
        dx = jnp.where(j == 0, 2, jnp.where(j == 1, 1, jnp.where(j == 2, 3, 0)))
        return (z + 1 - i % 2) % 2, (x + dx) % 4

    def near_first(n, zz, xx, sg):
        dx = jnp.where(n < 4, jnp.where(n % 2 == 0, -sg, 0), jnp.where(n % 2 == 0, sg, 2 * sg))
        return (zz + 1 - (n // 2) % 2) % 2, (xx + dx + 4) % 4

    barrier = pltpu.get_barrier_semaphore()
    for k in range(NF - 1):
        pl.semaphore_signal(barrier, inc=1, device_id={"frames": peer(f, k)}, device_id_type=MESH)
    for k in range(1, NR):
        pl.semaphore_signal(barrier, inc=1, device_id={"rows": (r + k) % NR}, device_id_type=MESH)
    nz_load = pltpu.make_async_copy(noise.at[:, pl.ds(2, 3)], nz, osem.at[4])
    nz_load.start()
    loads = [pltpu.make_async_copy(video.at[k], vv.at[k], lsem.at[k]) for k in range(2)]
    for cp in loads:
        cp.start()
    w3[0:256] = wt[2 - 2 * c]
    w3[256:512] = wt[1]
    w3[512:768] = wt[2 * c]

    @pl.when(is_end)
    def _():
        halo[...] = jnp.zeros(halo.shape, BF)

    for axis_at, ref in ((r, tb), (f, ed)):
        count = NR if ref is tb else NF
        for side, edge in ((0, 0), (1, count - 1)):
            @pl.when(axis_at == edge)
            def _():
                ref[side] = jnp.zeros(ref.shape[1:], BF)

    st_e[...] = jnp.zeros(st_e.shape, F32)
    st_l[...] = jnp.zeros(st_l.shape, F32)
    pl.semaphore_wait(barrier, NF + NR - 2)

    is_mid = (f == NF // 2 - 1) | (f == NF // 2)

    def halo_copy(n):
        zz, xx = near_first(n, outer_dev // 8, (x + sgn + 4) % 4, -sgn)
        return pltpu.make_async_remote_copy(
            src_ref=video.at[:, :, column(zz, xx)], dst_ref=halo.at[n], send_sem=hs.at[n], recv_sem=hr.at[n],
            device_id={"frames": outer_dev}, device_id_type=MESH)

    def detour_copy(n):
        zz, xx = near_first(n, outer_dev // 8, (x + sgn + 4) % 4, -sgn)
        return pltpu.make_async_remote_copy(
            src_ref=video.at[:, :, column(zz, xx)], dst_ref=relay.at[n - 2], send_sem=ls.at[n - 2], recv_sem=lr.at[n - 2],
            device_id={"frames": jnp.where(f < NF // 2, NF - 1, 0)}, device_id_type=MESH)

    def relay_copy(n):
        return pltpu.make_async_remote_copy(
            src_ref=relay.at[n - 2], dst_ref=halo.at[n], send_sem=hs.at[n], recv_sem=hr.at[n],
            device_id={"frames": jnp.where(f < NF // 2, NF // 2 - 1, NF // 2)}, device_id_type=MESH)

    def inner_copy(i):
        zz, xx = far_first(i)
        return pltpu.make_async_remote_copy(
            src_ref=video.at[inner_frame, :, column(zz, xx)], dst_ref=inner.at[i], send_sem=ns.at[i], recv_sem=nr.at[i],
            device_id={"frames": inner_dev}, device_id_type=MESH)

    for i in range(8):
        inner_copy(i).start()

    def halo_start(blocks):
        for n in blocks:
            if n < 2:
                @pl.when(not_end)
                def _():
                    halo_copy(n).start()
            else:
                @pl.when(not_end & jnp.logical_not(is_mid))
                def _():
                    halo_copy(n).start()

    @pl.when(is_mid)
    def _():
        for n in (2, 3):
            detour_copy(n).start()

    halo_start(HALO_AT[0])

    for cp in loads:
        cp.wait()

    def inner_send(i, dc):
        zz, xx = far_first(i)
        dest = zz * 8 + xx * 2 + (c + dc) % 2
        slot = 2 * i + dc
        return pltpu.make_async_remote_copy(
            src_ref=si.at[i, (c + dc) % 2], dst_ref=pb.at[chip, 2 + c], send_sem=is_.at[slot], recv_sem=ir.at[slot],
            device_id={"frames": dest}, device_id_type=MESH)

    def inner_block(i, carry):
        zz, xx = far_first(i)
        wait_in(inner.at[i], nr.at[i])
        here = column(zz, xx)
        proj = temporal(inner[i], vv[inner_frame, :, here], vv[outer_frame, :, here], w3, wp)
        for h in range(2):
            si[i, h] = proj[:, h]
        inner_send(i, 1).start()

        @pl.when(i < 7)
        def _():
            inner_send(i, 0).start()

        return carry

    lax.fori_loop(0, 8, inner_block, 0)
    own_inner = pltpu.make_async_copy(si.at[7, c], pb.at[chip, 2 + c], lsem.at[0])
    own_inner.start()

    def outer_send(n, dc):
        zz, xx = near_first(n, z, x, sgn)
        dest = zz * 8 + xx * 2 + (c + dc) % 2
        slot = 2 * n + dc
        return pltpu.make_async_remote_copy(
            src_ref=so.at[n, (c + dc) % 2], dst_ref=pb.at[chip + c, pl.ds(0, 2)], send_sem=os.at[slot], recv_sem=or_.at[slot],
            device_id={"frames": dest}, device_id_type=MESH)

    def outer_block(n, carry):
        zz, xx = near_first(n, z, x, sgn)
        here = column(zz, xx)
        at = n % 4

        @pl.when(not_end)
        def _():
            wait_in(halo.at[at], hr.at[at])

        proj = temporal(vv[inner_frame, :, here], vv[outer_frame, :, here], halo[at, 1 - c], w3, wp)
        for h in range(2):
            so[n, h, 1 - c] = proj[:, h]
        proj = temporal(vv[outer_frame, :, here], halo[at, 1 - c], halo[at, c], w3, wp)
        for h in range(2):
            so[n, h, c] = proj[:, h]
        outer_send(n, 1).start()

        @pl.when(n != 3)
        def _():
            outer_send(n, 0).start()

        return carry

    def outer_blocks(first, past):
        lax.fori_loop(first, past, outer_block, 0)

    halo_start(HALO_AT[1])

    @pl.when(is_end)
    def _():
        outer_blocks(4, 8)
        outer_blocks(0, 4)
        for n in (2, 3):
            wait_in(relay.at[n - 2], lr.at[n - 2])
            relay_copy(n).start()

    def blocks_not_end(first, past):
        @pl.when(not_end)
        def _():
            outer_blocks(first, past)

    blocks_not_end(0, 2)

    def both_ways(axis, at, up_refs, down_refs, ssem, rsem, base, act):
        count = lax.axis_size(axis)
        first, last = at == 0, at == count - 1
        up = pltpu.make_async_remote_copy(
            src_ref=up_refs[0], dst_ref=up_refs[1], send_sem=ssem.at[base], recv_sem=rsem.at[base],
            device_id={axis: jnp.maximum(at - 1, 0)}, device_id_type=MESH)
        down = pltpu.make_async_remote_copy(
            src_ref=down_refs[0], dst_ref=down_refs[1], send_sem=ssem.at[base + 1], recv_sem=rsem.at[base + 1],
            device_id={axis: jnp.minimum(at + 1, count - 1)}, device_id_type=MESH)

        @pl.when(jnp.logical_not(first))
        def _():
            if act == "start":
                up.start()
            else:
                up.wait_send()
                down.wait_recv()

        @pl.when(jnp.logical_not(last))
        def _():
            if act == "start":
                down.start()
            else:
                down.wait_send()
                up.wait_recv()

    def rows_copies(q, lo, base, act):
        part = (pl.ds(0, q), pl.ds(lo, 2))
        both_ways("rows", r, (pb.at[part + (0,)], tb.at[(1,) + part]), (pb.at[part + (7,)], tb.at[(0,) + part]), ts, tr, base, act)

    def side_copies(q, lo, base, act):
        part = (pl.ds(0, q), pl.ds(lo, 2))
        both_ways("frames", f, (eo.at[(0,) + part], ed.at[(1,) + part]), (eo.at[(1,) + part], ed.at[(0,) + part]), es, er, base, act)

    sub = lax.broadcasted_iota(jnp.int32, (8, 128), 0)

    def edges(lo):
        def body(q, carry):
            for k in (lo, lo + 1):
                for s in range(2):
                    cols = slice(16 * s, 16 * s + 16)
                    at = 15 * s
                    own = pb[q, k, :, cols].astype(F32)[:, at, :]
                    above = tb[0, q, k, cols].astype(F32)[at:at + 1]
                    below = tb[1, q, k, cols].astype(F32)[at:at + 1]
                    outside = jnp.where(sub == 0, above, below)
                    eo[s, q, k] = jnp.concatenate([own, outside], axis=0).astype(BF)
            return carry
        return body

    def add_sums(table, per, kinds):
        def body(q, carry):
            for i, (_, at, nxt) in enumerate(kinds):
                a = slot_of(q, at)
                v = pb[a[0], a[1]].reshape(256, 128)
                if nxt is not None:
                    b = slot_of(q, nxt)
                    v = v + pb[b[0], b[1]].reshape(256, 128)
                v = v.astype(F32)
                scale = 1.0 if nxt is None else 0.5
                row = pl.ds(per * q + i, 1)
                table[0, row] = scale * jnp.sum(v, axis=0, keepdims=True)
                table[1, row] = scale * scale * jnp.sum(v * v, axis=0, keepdims=True)
            return carry
        lax.fori_loop(0, 8, body, 0)

    def reduce_rows(table, s1, r1, sem):
        half = table.shape[1] // 2
        s1[...] = gather_groups([table[k // 2, half * (k % 2):half * (k % 2) + half] for k in range(4)])
        copies = []
        for k in range(1, NR):
            cp = pltpu.make_async_remote_copy(
                src_ref=s1, dst_ref=r1.at[k - 1], send_sem=sem.at[0, k - 1], recv_sem=sem.at[1, k - 1],
                device_id={"rows": (r + k) % NR}, device_id_type=MESH)
            cp.start()
            copies.append(cp)
        return copies

    def reduce_frames(copies, s1, r1, s2, r2, sem):
        for cp in copies:
            cp.wait()
        total = s1[...]
        for k in range(NR - 1):
            total += r1[k]
        s2[...] = total
        copies = []
        for k in range(NF - 1):
            cp = pltpu.make_async_remote_copy(
                src_ref=s2, dst_ref=r2.at[k], send_sem=sem.at[0, k], recv_sem=sem.at[1, k],
                device_id={"frames": peer(f, k)}, device_id_type=MESH)
            cp.start()
            copies.append(cp)
        return copies

    def statistics(copies, s2, r2, out):
        for cp in copies:
            cp.wait()
        total = s2[...]
        for k in range(NF - 1):
            total += r2[k]
        count = 64 * 512 * 4
        half = out.shape[1] // 2
        for k in range(2):
            mean = spread_groups(total, k) / count
            square = spread_groups(total, k + 2) / count
            out[0, half * k:half * k + half] = mean
            out[1, half * k:half * k + half] = lax.rsqrt(square - mean * mean + 1e-05)

    for i in range(8):
        for dc in range(2):
            if i < 7 or dc:
                wait_in(pb.at[0, 2], ir.at[2 * i + dc])
    own_inner.wait()
    rows_copies(8, 2, 0, "start")
    add_sums(st_e, E_ROWS, EARLY)
    early_copies = reduce_rows(st_e, s1e, r1e, sem_e1)
    fill_weights(ws, w0, w1)
    blocks_not_end(2, 4)
    own_outer = pltpu.make_async_copy(so.at[3, c], pb.at[chip + c, pl.ds(0, 2)], lsem.at[1])
    own_outer.start()
    rows_copies(8, 2, 0, "wait")
    lax.fori_loop(0, 8, edges(2), 0)
    side_copies(8, 2, 0, "start")
    early_copies = reduce_frames(early_copies, s1e, r1e, s2e, r2e, sem_e2)

    for n in range(8):
        for dc in range(2):
            if n == 3 and dc == 0:
                continue
            if n < 4:
                wait_in(pb.at[0, pl.ds(0, 2)], or_.at[2 * n + dc])
            else:
                from_c = (c + dc) % 2
                sg = 2 * from_c - 1
                from_x = (x - (sg if n % 2 == 0 else 2 * sg) + 4) % 4
                from_dev = ((z + 1 - (n // 2) % 2) % 2) * 8 + from_x * 2 + from_c

                @pl.when((from_dev == 0) | (from_dev == NF - 1))
                def _():
                    wait_in(pb.at[0, pl.ds(0, 2)], or_.at[2 * n + dc])
    own_outer.wait()
    rows_copies(9, 0, 2, "start")
    add_sums(st_l, L_ROWS, LATE)
    late_copies = reduce_rows(st_l, s1l, r1l, sem_l1)
    pb_copy = pltpu.make_async_copy(pb, pb_out, osem.at[0])
    pb_copy.start()
    side_copies(8, 2, 0, "wait")
    nz_load.wait()
    statistics(early_copies, s2e, r2e, stat_e)

    keeps = border_keeps(f, r)

    def early_conv(q, carry):
        for i, (_, at, nxt) in enumerate(EARLY):
            norm_frame(slot_of(q, at), nxt and slot_of(q, nxt), E_ROWS * q + i, i,
                       pb, tb, ed, stat_e, gain, bias, ea.at[i], ll, None, keeps)
        rows = conv_rows(3, ll, w0, w1)
        for R in range(8):
            for i, (_, at, nxt) in enumerate(EARLY):
                v = pb[q, at[1], R]
                if nxt is not None:
                    v = v + pb[q, nxt[1], R]
                v = v.astype(F32) * (1.0 if nxt is None else 0.5)
                res_e[q, i, R] = (rows[R][i] + v + 0.3 * nz[q, i, R].astype(F32)).astype(BF)
        return carry

    lax.fori_loop(0, 4, early_conv, 0)
    late_copies = reduce_frames(late_copies, s1l, r1l, s2l, r2l, sem_l2)
    rows_copies(9, 0, 2, "wait")
    lax.fori_loop(0, 9, edges(0), 0)
    side_copies(9, 0, 2, "start")
    tb_copy = pltpu.make_async_copy(tb, tb_out, osem.at[1])
    tb_copy.start()
    lax.fori_loop(4, 8, early_conv, 0)
    early_copy = pltpu.make_async_copy(res_e, early_out, osem.at[3])
    early_copy.start()

    for i in range(8):
        inner_copy(i).wait_send()
        inner_send(i, 1).wait_send()
        if i < 7:
            inner_send(i, 0).wait_send()
    for n in range(4):
        outer_send(n, 1).wait_send()
        if n != 3:
            outer_send(n, 0).wait_send()

    @pl.when(not_end)
    def _():
        for n in range(2):
            halo_copy(n).wait_send()

    for n in range(2, 4):
        @pl.when(is_mid)
        def _():
            detour_copy(n).wait_send()

        @pl.when(jnp.logical_not(is_mid))
        def _():
            halo_copy(n).wait_send()

    @pl.when(is_end)
    def _():
        for n in range(4, 8):
            outer_send(n, 1).wait_send()
            outer_send(n, 0).wait_send()

    side_copies(9, 0, 2, "wait")
    ed_copy = pltpu.make_async_copy(ed, ed_out, osem.at[2])
    ed_copy.start()
    statistics(late_copies, s2l, r2l, st_out)
    pb_copy.wait()
    tb_copy.wait()
    ed_copy.wait()
    early_copy.wait()


def local(video, w_time, w_proj, w_space, gn_gain, gn_bias, noise):
    slots = 2 * NF + 4
    full = lambda shape: pl.BlockSpec(shape, lambda g: (0,) * len(shape))
    anyw = pl.BlockSpec(memory_space=pl.ANY)
    vm = pl.BlockSpec(memory_space=pltpu.VMEM)
    quads = slots // 4
    dma = pltpu.SemaphoreType.DMA
    gain, bias = gn_gain.reshape(1, 128), gn_bias.reshape(1, 128)
    pb, tb, ed, st, early = pl.pallas_call(
        move_kernel,
        out_shape=(
            jax.ShapeDtypeStruct((quads, 4, 8, 32, 128), BF),
            jax.ShapeDtypeStruct((2, quads, 4, 32, 128), BF),
            jax.ShapeDtypeStruct((2, quads, 4, 16, 128), BF),
            jax.ShapeDtypeStruct((2, 8 * L_ROWS, 128), F32),
            jax.ShapeDtypeStruct((8, 3, 8, 32, 128), BF),
        ),
        in_specs=[anyw, vm, vm, vm, vm, vm, anyw],
        out_specs=(anyw, anyw, anyw, vm, anyw),
        scratch_shapes=[
            pltpu.VMEM((2, 8, 512, 256), BF),
            pltpu.VMEM((8, 8, 64, 256), BF),
            pltpu.VMEM((4, 2, 8, 64, 256), BF),
            pltpu.VMEM((2, 2, 8, 64, 256), BF),
            pltpu.VMEM((768, 256), BF),
            pltpu.VMEM((8, 2, 8, 32, 128), BF),
            pltpu.VMEM((8, 2, 2, 8, 32, 128), BF),
            pltpu.VMEM((quads, 4, 8, 32, 128), BF),
            pltpu.VMEM((2, quads, 4, 32, 128), BF),
            pltpu.VMEM((2, quads, 4, 16, 128), BF),
            pltpu.VMEM((2, quads, 4, 16, 128), BF),
            pltpu.VMEM((2, 8 * E_ROWS, 128), F32),
            pltpu.VMEM((4 * E_ROWS, 128), F32),
            pltpu.VMEM((NR - 1, 4 * E_ROWS, 128), F32),
            pltpu.VMEM((4 * E_ROWS, 128), F32),
            pltpu.VMEM((NF - 1, 4 * E_ROWS, 128), F32),
            pltpu.VMEM((2, 8 * E_ROWS, 128), F32),
            pltpu.VMEM((2, 8 * L_ROWS, 128), F32),
            pltpu.VMEM((4 * L_ROWS, 128), F32),
            pltpu.VMEM((NR - 1, 4 * L_ROWS, 128), F32),
            pltpu.VMEM((4 * L_ROWS, 128), F32),
            pltpu.VMEM((NF - 1, 4 * L_ROWS, 128), F32),
            pltpu.VMEM((8, 3, 8, 32, 128), BF),
            pltpu.VMEM((768, 256), BF),
            pltpu.VMEM((768, 256), BF),
            pltpu.VMEM((5, 96, 768), BF),
            pltpu.VMEM((3, 2, 16, 128), F32),
            pltpu.VMEM((8, 3, 8, 32, 128), BF),
            dma((2,)),
            dma((8,)), dma((8,)),
            dma((4,)), dma((4,)),
            dma((2,)), dma((2,)),
            dma((16,)), dma((16,)),
            dma((16,)), dma((16,)),
            dma((4,)), dma((4,)),
            dma((4,)), dma((4,)),
            dma((2, NR - 1)), dma((2, NF - 1)),
            dma((2, NR - 1)), dma((2, NF - 1)),
            dma((5,)),
        ],
        compiler_params=pltpu.CompilerParams(collective_id=0, has_side_effects=True, vmem_limit_bytes=60 << 20),
        name="move",
    )(video, w_time, w_proj, w_space, gain, bias, noise.reshape(8, 8, 8, 32, 128))
    return pl.pallas_call(
        conv_kernel,
        grid=(9,),
        out_shape=jax.ShapeDtypeStruct((64, 8, 32, 128), BF),
        in_specs=[
            full((quads, 4, 8, 32, 128)), full((2, quads, 4, 32, 128)), full((2, quads, 4, 16, 128)), full((2, 8 * L_ROWS, 128)),
            pl.BlockSpec((1, 3, 8, 32, 128), lambda g: (jnp.maximum(g - 1, 0), 0, 0, 0, 0)),
            full((3, 3, 128, 128)), full((1, 128)), full((1, 128)),
            pl.BlockSpec((8, 8, 32, 128), lambda g: (jnp.maximum(g - 1, 0), 0, 0, 0)),
        ],
        out_specs=pl.BlockSpec((8, 8, 32, 128), lambda g: (jnp.maximum(g - 1, 0), 0, 0, 0)),
        scratch_shapes=[
            pltpu.VMEM((768, 256), BF),
            pltpu.VMEM((768, 256), BF),
            pltpu.VMEM((5, 160, 768), BF),
            pltpu.VMEM((5, 160, 768), BF),
            pltpu.VMEM((5, 8, 32, 128), BF),
            pltpu.VMEM((5, 8, 32, 128), BF),
            pltpu.VMEM((5, 2, 16, 128), F32),
        ],
        compiler_params=pltpu.CompilerParams(vmem_limit_bytes=60 << 20),
        name="conv",
    )(pb, tb, ed, st, early, w_space, gain, bias, noise)


def solution(mesh):
    in_specs = (
        P("frames", "rows", None, None),
        P(), P(), P(), P(), P(),
        P(None, "rows", "frames", None),
    )
    out_specs = P(None, "rows", "frames", None)
    return jax.shard_map(local, mesh=mesh, in_specs=in_specs, out_specs=out_specs, check_vma=False)
```

profile of v0, /device:TPU:1, one launch (start us, length us, event | category | flops | bytes accessed | tf_op | source)
XLA Modules:
  0.0 86.9 jit_solution(460189083046025915)
XLA Ops:
  0.0 75.1 %move.1 = (bf16[9,4,8,32,128]{4,3,2,1,0:T(8,128)(2,1)}, bf16[2,9,4,32,128]{4,3,2,1,0:T(8,128)(2,1)}, bf16[2,9,4,16,128]{4,3,2,1,0:T(8,128)(2,1)}, f32[2,48,128]{2,1,0:T(8,128)}, bf16[8,3,8,32,128]{4,3,2,1,0:T(8,128)(2,1)}) custom-call(bf16[2,8,512,256]{3,2,1,0:T(8,128)(2,1)} %video.1, bf16[3,256,256]{2,1,0:T(8,128)(2,1)} %wt.1, bf16[256,128]{1,0:T(8,128)(2,1)} %wp.1, ...), custom_call_target="tpu_custom_call" | custom-call | tf_op jit(solution)/shard_map/move/pallas_call | solution.py:588
  75.1 11.8 %conv.1 = bf16[64,8,32,128]{3,2,1,0:T(8,128)(2,1)} custom-call(bf16[9,4,8,32,128]{4,3,2,1,0:T(8,128)(2,1)} %get-tuple-element.10.pb, bf16[2,9,4,32,128]{4,3,2,1,0:T(8,128)(2,1)} %get-tuple-element.11.tb, bf16[2,9,4,16,128]{4,3,2,1,0:T(8,128)(2,1)} %get-tuple-element.12.ed, f32[2,48,128]{2,1,0:T(8,128)} %get-tuple-element.13.st, ...), custom_call_target="tpu_custom_call" | custom-call | tf_op jit(solution)/shard_map/conv/pallas_call | solution.py:643
where the time goes:
time: 87.2 us; the launch traced here: 86.9 us
  Pallas kernels  86.9 us (100%)
    pallas_call x1, Pallas kernels, local(): pl.pallas_call(move_kernel, out_shape=(jax.ShapeDtypeStruct((quads, 4, 8,...  75.1 us
    pallas_call x1, Pallas kernels, local(): pl.pallas_call(conv_kernel, grid=(9,), out_shape=jax.ShapeDtypeStruct((64...  11.8 us

commit v1 on v0

--- a/solution.py
+++ b/solution.py
@@ -115,54 +115,92 @@
             for R in range(8)]
 
 
-def conv_kernel(pb, tb, ed, st, early, ws, gain, bias, noise, out, w0, w1, ll_a, ll_b, fld_a, fld_b, ea):
+def conv_kernel(
+    pb_in, tb_in, ed_in, st, early, ws_in, gain, bias, noise, out,
+    pb, tb, ed, ws, nz, res, w0, w1, ll_a, ll_b, fld_a, fld_b, ea, qsem, nsem, osem, wsem,
+):
     f, r = lax.axis_index("frames"), lax.axis_index("rows")
-    g = pl.program_id(0)
-    steps = pl.num_programs(0) - 1
     keeps = border_keeps(f, r)
-
-    @pl.when(g == 0)
-    def _():
-        fill_weights(ws, w0, w1)
-
-    def step(new, old):
+    steps = noise.shape[0]
+
+    def quad_loads(k):
+        lo, n = ((0, 2), (2, 2), (4, 5))[k]
+        at = pl.ds(lo, n)
+        return [pltpu.make_async_copy(pb_in.at[at], pb.at[at], qsem.at[k, 0]),
+                pltpu.make_async_copy(tb_in.at[:, at], tb.at[:, at], qsem.at[k, 1]),
+                pltpu.make_async_copy(ed_in.at[:, at], ed.at[:, at], qsem.at[k, 2])]
+
+    def frame_loads(k):
+        lo, n = ((0, 2), (2, 6))[k]
+        at = pl.ds(lo, n)
+        return [pltpu.make_async_copy(noise.at[at, pl.ds(0, 2)], nz.at[at, pl.ds(0, 2)], nsem.at[k, 0]),
+                pltpu.make_async_copy(noise.at[at, pl.ds(5, 3)], nz.at[at, pl.ds(2, 3)], nsem.at[k, 1]),
+                pltpu.make_async_copy(early.at[at], res.at[at, pl.ds(2, 3)], nsem.at[k, 2])]
+
+    def store(q):
+        return pltpu.make_async_copy(res.at[q], out.at[q], osem.at[q])
+
+    weights = pltpu.make_async_copy(ws_in, ws, wsem)
+    for cp in quad_loads(0) + [weights]:
+        cp.start()
+
+    def step(g, new, old):
         if new is not None:
             ll, fld = new
             for i, (_, at, nxt) in enumerate(LATE):
                 norm_frame(slot_of(g, at), nxt and slot_of(g, nxt), L_ROWS * g + i, i,
                            pb, tb, ed, st, gain, bias, ea.at[i], ll, fld, keeps)
         if old is not None:
+            h = g - 1
             ll, fld = old
             rows = conv_rows(len(LATE), ll, w0, w1)
             for R in range(8):
                 for i, (k, _, nxt) in enumerate(LATE):
                     v = fld[i, R].astype(F32) * (1.0 if nxt is None else 0.5)
-                    out[k, R] = (rows[R][i] + v + 0.3 * noise[k, R].astype(F32)).astype(BF)
-            for i, (k, _, _) in enumerate(EARLY):
-                out[k] = early[0, i]
+                    res[h, k, R] = (rows[R][i] + v + 0.3 * nz[h, i, R].astype(F32)).astype(BF)
 
     a, b = (ll_a, fld_a), (ll_b, fld_b)
-
-    @pl.when(g == 0)
-    def _():
-        step(a, None)
-
-    @pl.when((g > 0) & (g < steps) & (g % 2 == 0))
-    def _():
-        step(a, b)
-
-    @pl.when((g < steps) & (g % 2 == 1))
-    def _():
-        step(b, a)
-
-    @pl.when(g == steps)
-    def _():
-        step(None, b)
+    for cp in quad_loads(0):
+        cp.wait()
+    for cp in quad_loads(1) + frame_loads(0):
+        cp.start()
+    step(0, a, None)
+    weights.wait()
+    fill_weights(ws, w0, w1)
+
+    def pair(i, carry):
+        for k in range(2):
+            @pl.when(i == k)
+            def _():
+                for cp in quad_loads(k + 1) + frame_loads(k):
+                    cp.wait()
+                if k == 0:
+                    for cp in quad_loads(2) + frame_loads(1):
+                        cp.start()
+
+        @pl.when(i > 0)
+        def _():
+            for k in range(2):
+                store(2 * i - 2 + k).start()
+
+        step(2 * i + 1, b, a)
+        step(2 * i + 2, a, b)
+        return carry
+
+    lax.fori_loop(0, steps // 2 - 1, pair, 0)
+    for q in range(steps - 4, steps - 2):
+        store(q).start()
+    step(steps - 1, b, a)
+    store(steps - 2).start()
+    step(steps, None, b)
+    store(steps - 1).start()
+    for q in range(steps):
+        store(q).wait()
 
 
 EARLY = ((2, (0, 2), None), (3, (0, 2), (0, 3)), (4, (0, 3), None))
 LATE = ((0, (0, 1), None), (1, (0, 1), (0, 2)), (5, (0, 3), (1, 0)), (6, (1, 0), None), (7, (1, 0), (1, 1)))
-HALO_AT = ((0, 1), (2, 3))
+HALO_AT = ((0,), (1, 2, 3))
 E_ROWS, L_ROWS = 4, 6
 
 
@@ -173,11 +211,11 @@
 
 
 def move_kernel(
-    video, wt, wp, ws, gain, bias, noise, pb_out, tb_out, ed_out, st_out, early_out,
-    vv, inner, halo, relay, w3, si, so, pb, tb, eo, ed,
+    video, wt_in, wp_in, ws_in, gain_in, bias_in, noise, pb_out, tb_out, ed_out, st_out, early_out,
+    wt, wp, ws, gain, bias, vv, inner, halo, relay, w3, si, so, pb, tb, eo, ed,
     st_e, s1e, r1e, s2e, r2e, stat_e, st_l, s1l, r1l, s2l, r2l,
     nz, w0, w1, ll, ea, res_e,
-    lsem, ns, nr, hs, hr, ls, lr, is_, ir, os, or_, ts, tr, es, er, sem_e1, sem_e2, sem_l1, sem_l2, osem,
+    lsem, ns, nr, hs, hr, ls, lr, is_, ir, os, or_, ts, tr, es, er, sem_e1, sem_e2, sem_l1, sem_l2, osem, wsem,
 ):
     f, r = lax.axis_index("frames"), lax.axis_index("rows")
     z, x, c = f // 8, (f // 2) % 4, f % 2
@@ -214,6 +252,12 @@
     loads = [pltpu.make_async_copy(video.at[k], vv.at[k], lsem.at[k]) for k in range(2)]
     for cp in loads:
         cp.start()
+    small = [pltpu.make_async_copy(a, b, wsem.at[k]) for k, (a, b) in enumerate(
+        ((wt_in, wt), (wp_in, wp), (ws_in, ws), (gain_in, gain), (bias_in, bias)))]
+    for cp in small:
+        cp.start()
+    for cp in small[:2]:
+        cp.wait()
     w3[0:256] = wt[2 - 2 * c]
     w3[256:512] = wt[1]
     w3[512:768] = wt[2 * c]
@@ -229,6 +273,8 @@
             def _():
                 ref[side] = jnp.zeros(ref.shape[1:], BF)
 
+    pb[0, 0] = jnp.zeros(pb.shape[2:], BF)
+    pb[8, 1] = jnp.zeros(pb.shape[2:], BF)
     st_e[...] = jnp.zeros(st_e.shape, F32)
     st_l[...] = jnp.zeros(st_l.shape, F32)
     pl.semaphore_wait(barrier, NF + NR - 2)
@@ -309,13 +355,27 @@
     own_inner = pltpu.make_async_copy(si.at[7, c], pb.at[chip, 2 + c], lsem.at[0])
     own_inner.start()
 
-    def outer_send(n, dc):
+    def outer_send(n, dc, alone):
         zz, xx = near_first(n, z, x, sgn)
         dest = zz * 8 + xx * 2 + (c + dc) % 2
         slot = 2 * n + dc
+        src, dst = so.at[n, (c + dc) % 2], pb.at[chip + c]
+        at = 1 - c if alone else pl.ds(0, 2)
         return pltpu.make_async_remote_copy(
-            src_ref=so.at[n, (c + dc) % 2], dst_ref=pb.at[chip + c, pl.ds(0, 2)], send_sem=os.at[slot], recv_sem=or_.at[slot],
+            src_ref=src.at[at], dst_ref=dst.at[at], send_sem=os.at[slot], recv_sem=or_.at[slot],
             device_id={"frames": dest}, device_id_type=MESH)
+
+    def outer_part(n, dc, act):
+        @pl.when(is_end)
+        def _():
+            cp = outer_send(n, dc, True)
+            cp.start() if act == "start" else cp.wait_send()
+
+        if not (isinstance(n, int) and n > 3):
+            @pl.when(not_end)
+            def _():
+                cp = outer_send(n, dc, False)
+                cp.start() if act == "start" else cp.wait_send()
 
     def outer_block(n, carry):
         zz, xx = near_first(n, z, x, sgn)
@@ -329,14 +389,18 @@
         proj = temporal(vv[inner_frame, :, here], vv[outer_frame, :, here], halo[at, 1 - c], w3, wp)
         for h in range(2):
             so[n, h, 1 - c] = proj[:, h]
-        proj = temporal(vv[outer_frame, :, here], halo[at, 1 - c], halo[at, c], w3, wp)
-        for h in range(2):
-            so[n, h, c] = proj[:, h]
-        outer_send(n, 1).start()
+
+        @pl.when(not_end)
+        def _():
+            proj = temporal(vv[outer_frame, :, here], halo[at, 1 - c], halo[at, c], w3, wp)
+            for h in range(2):
+                so[n, h, c] = proj[:, h]
+
+        outer_part(n, 1, "start")
 
         @pl.when(n != 3)
         def _():
-            outer_send(n, 0).start()
+            outer_part(n, 0, "start")
 
         return carry
 
@@ -476,31 +540,54 @@
     rows_copies(8, 2, 0, "start")
     add_sums(st_e, E_ROWS, EARLY)
     early_copies = reduce_rows(st_e, s1e, r1e, sem_e1)
+    for cp in small[2:]:
+        cp.wait()
     fill_weights(ws, w0, w1)
-    blocks_not_end(2, 4)
-    own_outer = pltpu.make_async_copy(so.at[3, c], pb.at[chip + c, pl.ds(0, 2)], lsem.at[1])
-    own_outer.start()
+    blocks_not_end(2, 3)
     rows_copies(8, 2, 0, "wait")
     lax.fori_loop(0, 8, edges(2), 0)
     side_copies(8, 2, 0, "start")
     early_copies = reduce_frames(early_copies, s1e, r1e, s2e, r2e, sem_e2)
+    blocks_not_end(3, 4)
+    own_pair = pltpu.make_async_copy(so.at[3, c], pb.at[chip + c, pl.ds(0, 2)], lsem.at[1])
+    own_frame = pltpu.make_async_copy(so.at[3, c, 1 - c], pb.at[chip + c, 1 - c], lsem.at[1])
+
+    @pl.when(not_end)
+    def _():
+        own_pair.start()
+
+    @pl.when(is_end)
+    def _():
+        own_frame.start()
+
 
     for n in range(8):
         for dc in range(2):
             if n == 3 and dc == 0:
                 continue
+            from_c = (c + dc) % 2
+            sg = 2 * from_c - 1
+            dx = (sg * (1 + n % 2)) if n > 3 else -sg if n % 2 == 0 else 0
+            from_dev = ((z + 1 - (n // 2) % 2) % 2) * 8 + ((x - dx + 4) % 4) * 2 + from_c
+            from_end = (from_dev == 0) | (from_dev == NF - 1)
+
+            @pl.when(from_end)
+            def _():
+                wait_in(pb.at[0, 0], or_.at[2 * n + dc])
+
             if n < 4:
-                wait_in(pb.at[0, pl.ds(0, 2)], or_.at[2 * n + dc])
-            else:
-                from_c = (c + dc) % 2
-                sg = 2 * from_c - 1
-                from_x = (x - (sg if n % 2 == 0 else 2 * sg) + 4) % 4
-                from_dev = ((z + 1 - (n // 2) % 2) % 2) * 8 + from_x * 2 + from_c
-
-                @pl.when((from_dev == 0) | (from_dev == NF - 1))
+                @pl.when(jnp.logical_not(from_end))
                 def _():
                     wait_in(pb.at[0, pl.ds(0, 2)], or_.at[2 * n + dc])
-    own_outer.wait()
+
+    @pl.when(not_end)
+    def _():
+        own_pair.wait()
+
+    @pl.when(is_end)
+    def _():
+        own_frame.wait()
+
     rows_copies(9, 0, 2, "start")
     add_sums(st_l, L_ROWS, LATE)
     late_copies = reduce_rows(st_l, s1l, r1l, sem_l1)
@@ -543,9 +630,9 @@
         if i < 7:
             inner_send(i, 0).wait_send()
     for n in range(4):
-        outer_send(n, 1).wait_send()
+        outer_part(n, 1, "wait")
         if n != 3:
-            outer_send(n, 0).wait_send()
+            outer_part(n, 0, "wait")
 
     @pl.when(not_end)
     def _():
@@ -564,8 +651,8 @@
     @pl.when(is_end)
     def _():
         for n in range(4, 8):
-            outer_send(n, 1).wait_send()
-            outer_send(n, 0).wait_send()
+            outer_send(n, 1, True).wait_send()
+            outer_send(n, 0, True).wait_send()
 
     side_copies(9, 0, 2, "wait")
     ed_copy = pltpu.make_async_copy(ed, ed_out, osem.at[2])
@@ -579,12 +666,12 @@
 
 def local(video, w_time, w_proj, w_space, gn_gain, gn_bias, noise):
     slots = 2 * NF + 4
-    full = lambda shape: pl.BlockSpec(shape, lambda g: (0,) * len(shape))
     anyw = pl.BlockSpec(memory_space=pl.ANY)
     vm = pl.BlockSpec(memory_space=pltpu.VMEM)
     quads = slots // 4
     dma = pltpu.SemaphoreType.DMA
     gain, bias = gn_gain.reshape(1, 128), gn_bias.reshape(1, 128)
+    noise = noise.reshape(8, 8, 8, 32, 128)
     pb, tb, ed, st, early = pl.pallas_call(
         move_kernel,
         out_shape=(
@@ -594,9 +681,14 @@
             jax.ShapeDtypeStruct((2, 8 * L_ROWS, 128), F32),
             jax.ShapeDtypeStruct((8, 3, 8, 32, 128), BF),
         ),
-        in_specs=[anyw, vm, vm, vm, vm, vm, anyw],
+        in_specs=[anyw, anyw, anyw, anyw, anyw, anyw, anyw],
         out_specs=(anyw, anyw, anyw, vm, anyw),
         scratch_shapes=[
+            pltpu.VMEM((3, 256, 256), BF),
+            pltpu.VMEM((256, 128), BF),
+            pltpu.VMEM((3, 3, 128, 128), BF),
+            pltpu.VMEM((1, 128), F32),
+            pltpu.VMEM((1, 128), F32),
             pltpu.VMEM((2, 8, 512, 256), BF),
             pltpu.VMEM((8, 8, 64, 256), BF),
             pltpu.VMEM((4, 2, 8, 64, 256), BF),
@@ -636,22 +728,23 @@
             dma((2, NR - 1)), dma((2, NF - 1)),
             dma((2, NR - 1)), dma((2, NF - 1)),
             dma((5,)),
+            dma((5,)),
         ],
         compiler_params=pltpu.CompilerParams(collective_id=0, has_side_effects=True, vmem_limit_bytes=60 << 20),
         name="move",
-    )(video, w_time, w_proj, w_space, gain, bias, noise.reshape(8, 8, 8, 32, 128))
-    return pl.pallas_call(
+    )(video, w_time, w_proj, w_space, gain, bias, noise)
+    out = pl.pallas_call(
         conv_kernel,
-        grid=(9,),
-        out_shape=jax.ShapeDtypeStruct((64, 8, 32, 128), BF),
-        in_specs=[
-            full((quads, 4, 8, 32, 128)), full((2, quads, 4, 32, 128)), full((2, quads, 4, 16, 128)), full((2, 8 * L_ROWS, 128)),
-            pl.BlockSpec((1, 3, 8, 32, 128), lambda g: (jnp.maximum(g - 1, 0), 0, 0, 0, 0)),
-            full((3, 3, 128, 128)), full((1, 128)), full((1, 128)),
-            pl.BlockSpec((8, 8, 32, 128), lambda g: (jnp.maximum(g - 1, 0), 0, 0, 0)),
-        ],
-        out_specs=pl.BlockSpec((8, 8, 32, 128), lambda g: (jnp.maximum(g - 1, 0), 0, 0, 0)),
+        out_shape=jax.ShapeDtypeStruct((8, 8, 8, 32, 128), BF),
+        in_specs=[anyw, anyw, anyw, vm, anyw, anyw, vm, vm, anyw],
+        out_specs=anyw,
         scratch_shapes=[
+            pltpu.VMEM((quads, 4, 8, 32, 128), BF),
+            pltpu.VMEM((2, quads, 4, 32, 128), BF),
+            pltpu.VMEM((2, quads, 4, 16, 128), BF),
+            pltpu.VMEM((3, 3, 128, 128), BF),
+            pltpu.VMEM((8, 5, 8, 32, 128), BF),
+            pltpu.VMEM((8, 8, 8, 32, 128), BF),
             pltpu.VMEM((768, 256), BF),
             pltpu.VMEM((768, 256), BF),
             pltpu.VMEM((5, 160, 768), BF),
@@ -659,10 +752,12 @@
             pltpu.VMEM((5, 8, 32, 128), BF),
             pltpu.VMEM((5, 8, 32, 128), BF),
             pltpu.VMEM((5, 2, 16, 128), F32),
+            dma((3, 3)), dma((2, 3)), dma((8,)), dma,
         ],
         compiler_params=pltpu.CompilerParams(vmem_limit_bytes=60 << 20),
         name="conv",
     )(pb, tb, ed, st, early, w_space, gain, bias, noise)
+    return out.reshape(64, 8, 32, 128)
 
 
 def solution(mesh):

time: 87.2 us -> 80.8 us (0.927)
  Pallas kernels: 86.9 us -> 80.2 us
    pallas_call x1, Pallas kernels: 75.1 us -> 68.7 us  [local(): pl.pallas_call(move_kernel, out_shape=(jax.ShapeDtypeStruct((quads, 4, 8,...]
where the time goes in v1:
time: 80.8 us; the launch traced here: 80.2 us
  Pallas kernels  80.2 us (99%)
    pallas_call x1, Pallas kernels, local(): pl.pallas_call(move_kernel, out_shape=(jax.ShapeDtypeStruct((quads, 4, 8,...  68.7 us
    pallas_call x1, Pallas kernels, local(): pl.pallas_call(conv_kernel, out_shape=jax.ShapeDtypeStruct((8, 8, 8, 32,...  11.5 us

profile of v1, /device:TPU:1, one launch (start us, length us, event | category | flops | bytes accessed | tf_op | source)
XLA Modules:
  0.0 80.2 jit_solution(7109828728728489606)
XLA Ops:
  0.0 68.7 %move.1 = (bf16[9,4,8,32,128]{4,3,2,1,0:T(8,128)(2,1)}, bf16[2,9,4,32,128]{4,3,2,1,0:T(8,128)(2,1)}, bf16[2,9,4,16,128]{4,3,2,1,0:T(8,128)(2,1)}, f32[2,48,128]{2,1,0:T(8,128)}, bf16[8,3,8,32,128]{4,3,2,1,0:T(8,128)(2,1)}) custom-call(bf16[2,8,512,256]{3,2,1,0:T(8,128)(2,1)} %video.1, bf16[3,256,256]{2,1,0:T(8,128)(2,1)} %wt_in.1, bf16[256,128]{1,0:T(8,128)(2,1)} %wp_in.1, ...), custom_call_target="tpu_custom_call" | custom-call | tf_op jit(solution)/shard_map/move/pallas_call | solution.py:675
  68.7 11.5 %conv.1 = bf16[8,8,8,32,128]{4,3,2,1,0:T(8,128)(2,1)} custom-call(bf16[9,4,8,32,128]{4,3,2,1,0:T(8,128)(2,1)} %get-tuple-element.10.pb_in, bf16[2,9,4,32,128]{4,3,2,1,0:T(8,128)(2,1)} %get-tuple-element.11.tb_in, bf16[2,9,4,16,128]{4,3,2,1,0:T(8,128)(2,1)} %get-tuple-element.12.ed_in, f32[2,48,128]{2,1,0:T(8,128)} %get-tuple-element.13.st, ...), custom_call_target="tpu_custom_call" | custom-call | tf_op jit(solution)/shard_map/conv/pallas_call | solution.py:736

commit v2 on v1

--- a/solution.py
+++ b/solution.py
@@ -116,32 +116,38 @@
 
 
 def conv_kernel(
-    pb_in, tb_in, ed_in, st, early, ws_in, gain, bias, noise, out,
-    pb, tb, ed, ws, nz, res, w0, w1, ll_a, ll_b, fld_a, fld_b, ea, qsem, nsem, osem, wsem,
+    pb_in, tb_in, ed_in, st_in, early, ends, ws_in, gain_in, bias_in, noise, out,
+    st, gain, bias, pb, tb, ed, ws, nz, passing, passing_ends, r0, r1, r2, r3, r4, r5, r6,
+    w0, w1, ll_a, ll_b, fld_a, fld_b, ea, qsem, nsem, osem, psem, wsem, ssem,
 ):
     f, r = lax.axis_index("frames"), lax.axis_index("rows")
     keeps = border_keeps(f, r)
-    steps = noise.shape[0]
+    steps = 7
+    res = (r0, r1, r2, r3, r4, r5, r6)
 
     def quad_loads(k):
-        lo, n = ((0, 2), (2, 2), (4, 5))[k]
+        lo, n = ((0, 2), (2, 2), (4, 4))[k]
         at = pl.ds(lo, n)
         return [pltpu.make_async_copy(pb_in.at[at], pb.at[at], qsem.at[k, 0]),
                 pltpu.make_async_copy(tb_in.at[:, at], tb.at[:, at], qsem.at[k, 1]),
                 pltpu.make_async_copy(ed_in.at[:, at], ed.at[:, at], qsem.at[k, 2])]
 
     def frame_loads(k):
-        lo, n = ((0, 2), (2, 6))[k]
-        at = pl.ds(lo, n)
-        return [pltpu.make_async_copy(noise.at[at, pl.ds(0, 2)], nz.at[at, pl.ds(0, 2)], nsem.at[k, 0]),
-                pltpu.make_async_copy(noise.at[at, pl.ds(5, 3)], nz.at[at, pl.ds(2, 3)], nsem.at[k, 1]),
-                pltpu.make_async_copy(early.at[at], res.at[at, pl.ds(2, 3)], nsem.at[k, 2])]
-
-    def store(q):
-        return pltpu.make_async_copy(res.at[q], out.at[q], osem.at[q])
+        return [pltpu.make_async_copy(noise.at[pl.ds(8 * g + 5, 5)], nz.at[g], nsem.at[g])
+                for g in ((0, 1), (2, 3, 4, 5, 6))[k]]
+
+    early_load = [pltpu.make_async_copy(early, passing, psem.at[0]), pltpu.make_async_copy(ends, passing_ends, psem.at[1])]
+    early_store = [pltpu.make_async_copy(passing.at[q], out.at[pl.ds(8 * q + 2, 3)], psem.at[2 + q]) for q in range(8)]
+    early_store += [pltpu.make_async_copy(passing_ends.at[pl.ds(0, 2)], out.at[pl.ds(0, 2)], psem.at[10]),
+                    pltpu.make_async_copy(passing_ends.at[pl.ds(2, 3)], out.at[pl.ds(61, 3)], psem.at[11])]
+
+    def stores(g):
+        return [pltpu.make_async_copy(res[g], out.at[pl.ds(8 * g + 5, 5)], osem.at[g])]
 
     weights = pltpu.make_async_copy(ws_in, ws, wsem)
-    for cp in quad_loads(0) + [weights]:
+    small = [pltpu.make_async_copy(a, b, ssem.at[k]) for k, (a, b) in enumerate(
+        ((st_in, st), (gain_in, gain), (bias_in, bias)))]
+    for cp in small + quad_loads(0) + [weights]:
         cp.start()
 
     def step(g, new, old):
@@ -155,66 +161,58 @@
             ll, fld = old
             rows = conv_rows(len(LATE), ll, w0, w1)
             for R in range(8):
-                for i, (k, _, nxt) in enumerate(LATE):
+                for i, (_, _, nxt) in enumerate(LATE):
                     v = fld[i, R].astype(F32) * (1.0 if nxt is None else 0.5)
-                    res[h, k, R] = (rows[R][i] + v + 0.3 * nz[h, i, R].astype(F32)).astype(BF)
+                    res[h][i, R] = (rows[R][i] + v + 0.3 * nz[h, i, R].astype(F32)).astype(BF)
 
     a, b = (ll_a, fld_a), (ll_b, fld_b)
-    for cp in quad_loads(0):
-        cp.wait()
-    for cp in quad_loads(1) + frame_loads(0):
-        cp.start()
+    def arrive(copies):
+        for cp in copies:
+            cp.wait()
+
+    def start(copies):
+        for cp in copies:
+            cp.start()
+
+    arrive(small + quad_loads(0))
+    start(quad_loads(1) + frame_loads(0))
     step(0, a, None)
-    weights.wait()
+    arrive([weights])
     fill_weights(ws, w0, w1)
-
-    def pair(i, carry):
-        for k in range(2):
-            @pl.when(i == k)
-            def _():
-                for cp in quad_loads(k + 1) + frame_loads(k):
-                    cp.wait()
-                if k == 0:
-                    for cp in quad_loads(2) + frame_loads(1):
-                        cp.start()
-
-        @pl.when(i > 0)
-        def _():
-            for k in range(2):
-                store(2 * i - 2 + k).start()
-
-        step(2 * i + 1, b, a)
-        step(2 * i + 2, a, b)
-        return carry
-
-    lax.fori_loop(0, steps // 2 - 1, pair, 0)
-    for q in range(steps - 4, steps - 2):
-        store(q).start()
-    step(steps - 1, b, a)
-    store(steps - 2).start()
-    step(steps, None, b)
-    store(steps - 1).start()
+    for g in range(1, steps + 1):
+        if g == 1:
+            arrive(quad_loads(1) + frame_loads(0))
+            start(quad_loads(2) + frame_loads(1) + early_load)
+        if g == 3:
+            arrive(quad_loads(2) + frame_loads(1))
+        step(g, (a, b)[g % 2] if g < steps else None, (b, a)[g % 2])
+        if g > 1:
+            start(stores(g - 2))
+        if g == 5:
+            arrive(early_load)
+            start(early_store)
+    start(stores(steps - 1))
+    arrive(early_store)
     for q in range(steps):
-        store(q).wait()
+        arrive(stores(q))
 
 
 EARLY = ((2, (0, 2), None), (3, (0, 2), (0, 3)), (4, (0, 3), None))
-LATE = ((0, (0, 1), None), (1, (0, 1), (0, 2)), (5, (0, 3), (1, 0)), (6, (1, 0), None), (7, (1, 0), (1, 1)))
+LATE = ((5, (0, 3), (1, 0)), (6, (1, 0), None), (7, (1, 0), (1, 1)), (8, (1, 1), None), (9, (1, 1), (1, 2)))
+ENDS = (((0, 1), None), ((0, 1), (0, 2)), ((7, 3), (8, 0)), ((8, 0), None), ((8, 0), (8, 0)))
 HALO_AT = ((0,), (1, 2, 3))
 E_ROWS, L_ROWS = 4, 6
 
 
 def slot_of(q, at):
-    if at == (1, 1):
-        return q + 1, jnp.where(q == 7, 0, 1)
     return q + at[0], at[1]
 
 
 def move_kernel(
-    video, wt_in, wp_in, ws_in, gain_in, bias_in, noise, pb_out, tb_out, ed_out, st_out, early_out,
+    video, wt_in, wp_in, ws_in, gain_in, bias_in, noise, pb_out, tb_out, ed_out, st_out, early_out, ends_out,
     wt, wp, ws, gain, bias, vv, inner, halo, relay, w3, si, so, pb, tb, eo, ed,
     st_e, s1e, r1e, s2e, r2e, stat_e, st_l, s1l, r1l, s2l, r2l,
-    nz, w0, w1, ll, ea, res_e,
+    nz, w0, w1, ll, ea, res_e, nz_x, ll_x, res_x,
     lsem, ns, nr, hs, hr, ls, lr, is_, ir, os, or_, ts, tr, es, er, sem_e1, sem_e2, sem_l1, sem_l2, osem, wsem,
 ):
     f, r = lax.axis_index("frames"), lax.axis_index("rows")
@@ -247,8 +245,11 @@
         pl.semaphore_signal(barrier, inc=1, device_id={"frames": peer(f, k)}, device_id_type=MESH)
     for k in range(1, NR):
         pl.semaphore_signal(barrier, inc=1, device_id={"rows": (r + k) % NR}, device_id_type=MESH)
-    nz_load = pltpu.make_async_copy(noise.at[:, pl.ds(2, 3)], nz, osem.at[4])
-    nz_load.start()
+    nz_loads = [pltpu.make_async_copy(noise.at[:, pl.ds(2, 3)], nz, osem.at[4]),
+                pltpu.make_async_copy(noise.at[0, pl.ds(0, 2)], nz_x.at[pl.ds(0, 2)], osem.at[6]),
+                pltpu.make_async_copy(noise.at[7, pl.ds(5, 3)], nz_x.at[pl.ds(2, 3)], osem.at[7])]
+    for cp in nz_loads:
+        cp.start()
     loads = [pltpu.make_async_copy(video.at[k], vv.at[k], lsem.at[k]) for k in range(2)]
     for cp in loads:
         cp.start()
@@ -454,8 +455,13 @@
         part = (pl.ds(0, q), pl.ds(lo, 2))
         both_ways("rows", r, (pb.at[part + (0,)], tb.at[(1,) + part]), (pb.at[part + (7,)], tb.at[(0,) + part]), ts, tr, base, act)
 
-    def side_copies(q, lo, base, act):
-        part = (pl.ds(0, q), pl.ds(lo, 2))
+    def pair_rows(q, act):
+        part = (q, pl.ds(0, 2))
+        both_ways("rows", r, (pb.at[part + (0,)], tb.at[(1,) + part]), (pb.at[part + (7,)], tb.at[(0,) + part]),
+                  ts, tr, 2 + 2 * q, act)
+
+    def side_copies(first, q, lo, base, act):
+        part = (pl.ds(first, q), pl.ds(lo, 2))
         both_ways("frames", f, (eo.at[(0,) + part], ed.at[(1,) + part]), (eo.at[(1,) + part], ed.at[(0,) + part]), es, er, base, act)
 
     sub = lax.broadcasted_iota(jnp.int32, (8, 128), 0)
@@ -474,21 +480,49 @@
             return carry
         return body
 
-    def add_sums(table, per, kinds):
-        def body(q, carry):
-            for i, (_, at, nxt) in enumerate(kinds):
-                a = slot_of(q, at)
-                v = pb[a[0], a[1]].reshape(256, 128)
-                if nxt is not None:
-                    b = slot_of(q, nxt)
-                    v = v + pb[b[0], b[1]].reshape(256, 128)
-                v = v.astype(F32)
-                scale = 1.0 if nxt is None else 0.5
-                row = pl.ds(per * q + i, 1)
-                table[0, row] = scale * jnp.sum(v, axis=0, keepdims=True)
-                table[1, row] = scale * scale * jnp.sum(v * v, axis=0, keepdims=True)
-            return carry
-        lax.fori_loop(0, 8, body, 0)
+    def add_sums(table, row, now, nxt):
+        v = pb[now].reshape(256, 128)
+        if nxt is not None:
+            v = v + pb[nxt].reshape(256, 128)
+        v = v.astype(F32)
+        scale = 1.0 if nxt is None else 0.5
+        row = pl.ds(row, 1)
+        table[0, row] = scale * jnp.sum(v, axis=0, keepdims=True)
+        table[1, row] = scale * scale * jnp.sum(v * v, axis=0, keepdims=True)
+
+    def early_sums(q, carry):
+        for i, (_, at, nxt) in enumerate(EARLY):
+            add_sums(st_e, E_ROWS * q + i, slot_of(q, at), nxt and slot_of(q, nxt))
+        return carry
+
+    def pair_arrived(q):
+        pair_rows(q, "start")
+        for i, (_, at, nxt) in enumerate(LATE):
+            add_sums(st_l, L_ROWS * (q - 1) + i, slot_of(q - 1, at), nxt and slot_of(q - 1, nxt))
+
+    def source_of(slot):
+        n, dc = slot // 2, slot % 2
+        from_c = (c + dc) % 2
+        sg = 2 * from_c - 1
+        dx = jnp.where(n > 3, sg * (1 + n % 2), jnp.where(n % 2 == 0, -sg, 0))
+        from_dev = ((z + 1 - (n // 2) % 2) % 2) * 8 + ((x - dx + 4) % 4) * 2 + from_c
+        return from_dev, (from_dev == 0) | (from_dev == NF - 1)
+
+    def end_arrival(slot, carry):
+        @pl.when(source_of(slot)[1] & (slot != 6))
+        def _():
+            wait_in(pb.at[0, 0], or_.at[slot])
+        return carry
+
+    def outer_arrival(slot, carry):
+        from_dev, from_end = source_of(slot)
+
+        @pl.when(jnp.logical_not(from_end) & (slot != 6))
+        def _():
+            wait_in(pb.at[0, pl.ds(0, 2)], or_.at[slot])
+            pair_arrived(from_dev // 2 + from_dev % 2)
+
+        return carry
 
     def reduce_rows(table, s1, r1, sem):
         half = table.shape[1] // 2
@@ -538,7 +572,19 @@
                 wait_in(pb.at[0, 2], ir.at[2 * i + dc])
     own_inner.wait()
     rows_copies(8, 2, 0, "start")
-    add_sums(st_e, E_ROWS, EARLY)
+    lax.fori_loop(0, 16, end_arrival, 0)
+
+    @pl.when(is_end)
+    def _():
+        own_frame = pltpu.make_async_copy(so.at[3, c, 1 - c], pb.at[chip + c, 1 - c], lsem.at[1])
+        own_frame.start()
+        own_frame.wait()
+
+    for q in (0, 8):
+        pair_rows(q, "start")
+    lax.fori_loop(0, 8, early_sums, 0)
+    for i, (at, nxt) in enumerate(ENDS):
+        add_sums(st_e, E_ROWS * i + 3, at, nxt)
     early_copies = reduce_rows(st_e, s1e, r1e, sem_e1)
     for cp in small[2:]:
         cp.wait()
@@ -546,55 +592,35 @@
     blocks_not_end(2, 3)
     rows_copies(8, 2, 0, "wait")
     lax.fori_loop(0, 8, edges(2), 0)
-    side_copies(8, 2, 0, "start")
+    side_copies(0, 8, 2, 0, "start")
+    for k, q in enumerate((0, 8)):
+        pair_rows(q, "wait")
+        edges(0)(q, 0)
+        side_copies(q, 1, 0, 4 + 2 * k, "start")
     early_copies = reduce_frames(early_copies, s1e, r1e, s2e, r2e, sem_e2)
     blocks_not_end(3, 4)
     own_pair = pltpu.make_async_copy(so.at[3, c], pb.at[chip + c, pl.ds(0, 2)], lsem.at[1])
-    own_frame = pltpu.make_async_copy(so.at[3, c, 1 - c], pb.at[chip + c, 1 - c], lsem.at[1])
 
     @pl.when(not_end)
     def _():
         own_pair.start()
 
-    @pl.when(is_end)
-    def _():
-        own_frame.start()
-
-
-    for n in range(8):
-        for dc in range(2):
-            if n == 3 and dc == 0:
-                continue
-            from_c = (c + dc) % 2
-            sg = 2 * from_c - 1
-            dx = (sg * (1 + n % 2)) if n > 3 else -sg if n % 2 == 0 else 0
-            from_dev = ((z + 1 - (n // 2) % 2) % 2) * 8 + ((x - dx + 4) % 4) * 2 + from_c
-            from_end = (from_dev == 0) | (from_dev == NF - 1)
-
-            @pl.when(from_end)
-            def _():
-                wait_in(pb.at[0, 0], or_.at[2 * n + dc])
-
-            if n < 4:
-                @pl.when(jnp.logical_not(from_end))
-                def _():
-                    wait_in(pb.at[0, pl.ds(0, 2)], or_.at[2 * n + dc])
+
+    lax.fori_loop(0, 8, outer_arrival, 0)
 
     @pl.when(not_end)
     def _():
         own_pair.wait()
-
-    @pl.when(is_end)
-    def _():
-        own_frame.wait()
-
-    rows_copies(9, 0, 2, "start")
-    add_sums(st_l, L_ROWS, LATE)
+        pair_arrived(chip + c)
+
     late_copies = reduce_rows(st_l, s1l, r1l, sem_l1)
     pb_copy = pltpu.make_async_copy(pb, pb_out, osem.at[0])
     pb_copy.start()
-    side_copies(8, 2, 0, "wait")
-    nz_load.wait()
+    side_copies(0, 8, 2, 0, "wait")
+    for k, q in enumerate((0, 8)):
+        side_copies(q, 1, 0, 4 + 2 * k, "wait")
+    for cp in nz_loads:
+        cp.wait()
     statistics(early_copies, s2e, r2e, stat_e)
 
     keeps = border_keeps(f, r)
@@ -615,14 +641,27 @@
 
     lax.fori_loop(0, 4, early_conv, 0)
     late_copies = reduce_frames(late_copies, s1l, r1l, s2l, r2l, sem_l2)
-    rows_copies(9, 0, 2, "wait")
-    lax.fori_loop(0, 9, edges(0), 0)
-    side_copies(9, 0, 2, "start")
+    for q in range(1, 8):
+        pair_rows(q, "wait")
+    lax.fori_loop(1, 8, edges(0), 0)
+    side_copies(1, 7, 0, 2, "start")
     tb_copy = pltpu.make_async_copy(tb, tb_out, osem.at[1])
     tb_copy.start()
     lax.fori_loop(4, 8, early_conv, 0)
+    for i, (at, nxt) in enumerate(ENDS):
+        norm_frame(at, nxt, E_ROWS * i + 3, i, pb, tb, ed, stat_e, gain, bias, ea.at[i], ll_x, None, keeps)
+    rows = conv_rows(5, ll_x, w0, w1)
+    for R in range(8):
+        for i, (at, nxt) in enumerate(ENDS):
+            v = pb[at[0], at[1], R]
+            if nxt is not None:
+                v = v + pb[nxt[0], nxt[1], R]
+            v = v.astype(F32) * (1.0 if nxt is None else 0.5)
+            res_x[i, R] = (rows[R][i] + v + 0.3 * nz_x[i, R].astype(F32)).astype(BF)
     early_copy = pltpu.make_async_copy(res_e, early_out, osem.at[3])
     early_copy.start()
+    ends_copy = pltpu.make_async_copy(res_x, ends_out, osem.at[5])
+    ends_copy.start()
 
     for i in range(8):
         inner_copy(i).wait_send()
@@ -654,7 +693,7 @@
             outer_send(n, 1, True).wait_send()
             outer_send(n, 0, True).wait_send()
 
-    side_copies(9, 0, 2, "wait")
+    side_copies(1, 7, 0, 2, "wait")
     ed_copy = pltpu.make_async_copy(ed, ed_out, osem.at[2])
     ed_copy.start()
     statistics(late_copies, s2l, r2l, st_out)
@@ -662,6 +701,7 @@
     tb_copy.wait()
     ed_copy.wait()
     early_copy.wait()
+    ends_copy.wait()
 
 
 def local(video, w_time, w_proj, w_space, gn_gain, gn_bias, noise):
@@ -672,7 +712,7 @@
     dma = pltpu.SemaphoreType.DMA
     gain, bias = gn_gain.reshape(1, 128), gn_bias.reshape(1, 128)
     noise = noise.reshape(8, 8, 8, 32, 128)
-    pb, tb, ed, st, early = pl.pallas_call(
+    pb, tb, ed, st, early, ends = pl.pallas_call(
         move_kernel,
         out_shape=(
             jax.ShapeDtypeStruct((quads, 4, 8, 32, 128), BF),
@@ -680,9 +720,10 @@
             jax.ShapeDtypeStruct((2, quads, 4, 16, 128), BF),
             jax.ShapeDtypeStruct((2, 8 * L_ROWS, 128), F32),
             jax.ShapeDtypeStruct((8, 3, 8, 32, 128), BF),
+            jax.ShapeDtypeStruct((5, 8, 32, 128), BF),
         ),
         in_specs=[anyw, anyw, anyw, anyw, anyw, anyw, anyw],
-        out_specs=(anyw, anyw, anyw, vm, anyw),
+        out_specs=(anyw, anyw, anyw, vm, anyw, anyw),
         scratch_shapes=[
             pltpu.VMEM((3, 256, 256), BF),
             pltpu.VMEM((256, 128), BF),
@@ -715,19 +756,22 @@
             pltpu.VMEM((768, 256), BF),
             pltpu.VMEM((768, 256), BF),
             pltpu.VMEM((5, 96, 768), BF),
-            pltpu.VMEM((3, 2, 16, 128), F32),
+            pltpu.VMEM((5, 2, 16, 128), F32),
             pltpu.VMEM((8, 3, 8, 32, 128), BF),
+            pltpu.VMEM((5, 8, 32, 128), BF),
+            pltpu.VMEM((5, 160, 768), BF),
+            pltpu.VMEM((5, 8, 32, 128), BF),
             dma((2,)),
             dma((8,)), dma((8,)),
             dma((4,)), dma((4,)),
             dma((2,)), dma((2,)),
             dma((16,)), dma((16,)),
             dma((16,)), dma((16,)),
-            dma((4,)), dma((4,)),
-            dma((4,)), dma((4,)),
+            dma((20,)), dma((20,)),
+            dma((8,)), dma((8,)),
             dma((2, NR - 1)), dma((2, NF - 1)),
             dma((2, NR - 1)), dma((2, NF - 1)),
-            dma((5,)),
+            dma((8,)),
             dma((5,)),
         ],
         compiler_params=pltpu.CompilerParams(collective_id=0, has_side_effects=True, vmem_limit_bytes=60 << 20),
@@ -735,16 +779,20 @@
     )(video, w_time, w_proj, w_space, gain, bias, noise)
     out = pl.pallas_call(
         conv_kernel,
-        out_shape=jax.ShapeDtypeStruct((8, 8, 8, 32, 128), BF),
-        in_specs=[anyw, anyw, anyw, vm, anyw, anyw, vm, vm, anyw],
+        out_shape=jax.ShapeDtypeStruct((64, 8, 32, 128), BF),
+        in_specs=[anyw] * 10,
         out_specs=anyw,
         scratch_shapes=[
+            pltpu.VMEM((2, 8 * L_ROWS, 128), F32),
+            pltpu.VMEM((1, 128), F32),
+            pltpu.VMEM((1, 128), F32),
             pltpu.VMEM((quads, 4, 8, 32, 128), BF),
             pltpu.VMEM((2, quads, 4, 32, 128), BF),
             pltpu.VMEM((2, quads, 4, 16, 128), BF),
             pltpu.VMEM((3, 3, 128, 128), BF),
             pltpu.VMEM((8, 5, 8, 32, 128), BF),
-            pltpu.VMEM((8, 8, 8, 32, 128), BF),
+            pltpu.VMEM((8, 3, 8, 32, 128), BF),
+            *[pltpu.VMEM((5, 8, 32, 128), BF)] * 8,
             pltpu.VMEM((768, 256), BF),
             pltpu.VMEM((768, 256), BF),
             pltpu.VMEM((5, 160, 768), BF),
@@ -752,12 +800,12 @@
             pltpu.VMEM((5, 8, 32, 128), BF),
             pltpu.VMEM((5, 8, 32, 128), BF),
             pltpu.VMEM((5, 2, 16, 128), F32),
-            dma((3, 3)), dma((2, 3)), dma((8,)), dma,
+            dma((3, 3)), dma((7,)), dma((7,)), dma((12,)), dma, dma((3,)),
         ],
         compiler_params=pltpu.CompilerParams(vmem_limit_bytes=60 << 20),
         name="conv",
-    )(pb, tb, ed, st, early, w_space, gain, bias, noise)
-    return out.reshape(64, 8, 32, 128)
+    )(pb, tb, ed, st, early, ends, w_space, gain, bias, noise.reshape(64, 8, 32, 128))
+    return out
 
 
 def solution(mesh):

time: 80.8 us -> 79.1 us (0.979)
  Pallas kernels: 80.2 us -> 78.8 us
    pallas_call x1, Pallas kernels: 11.5 us -> 10.2 us  [local(): pl.pallas_call(conv_kernel, out_shape=jax.ShapeDtypeStruct((64, 8, 32, 12...]
where the time goes in v2:
time: 79.1 us; the launch traced here: 78.9 us
  Pallas kernels  78.8 us (100%)
    pallas_call x1, Pallas kernels, local(): pl.pallas_call(move_kernel, out_shape=(jax.ShapeDtypeStruct((quads, 4, 8,...  68.5 us
    pallas_call x1, Pallas kernels, local(): pl.pallas_call(conv_kernel, out_shape=jax.ShapeDtypeStruct((64, 8, 32, 12...  10.2 us

profile of v2, /device:TPU:1, one launch (start us, length us, event | category | flops | bytes accessed | tf_op | source)
XLA Modules:
  0.0 78.9 jit_solution(5500191641048922002)
XLA Ops:
  0.0 68.5 %move.1 = (bf16[9,4,8,32,128]{4,3,2,1,0:T(8,128)(2,1)}, bf16[2,9,4,32,128]{4,3,2,1,0:T(8,128)(2,1)}, bf16[2,9,4,16,128]{4,3,2,1,0:T(8,128)(2,1)}, f32[2,48,128]{...) custom-call(bf16[2,8,512,256]{3,2,1,0:T(8,128)(2,1)} %video.1, ...), custom_call_target="tpu_custom_call" | custom-call | tf_op jit(solution)/shard_map/move/pallas_call | solution.py:715
  68.5 10.2 %conv.1 = bf16[64,8,32,128]{3,2,1,0:T(8,128)(2,1)} custom-call(bf16[9,4,8,32,128]{4,3,2,1,0:T(8,128)(2,1)} %get-tuple-element.11.pb_in, bf16[2,9,4,32,128]{4,3,2,1,0:T(8,128)(2,1)} %get-tuple-element.12.tb_in, bf16[2,9,4,16,128]{4,3,2,1,0:T(8,128)(2,1)} %get-tuple-element.13.ed_in, f32[2,48,128]{2,1,0:T(8,128)} %get-tuple-element.14.st_in, ...), custom_call_target="tpu_custom_call" | custom-call | tf_op jit(solution)/shard_map/conv/pallas_call | solution.py:780

commit v3 on v2

--- a/solution.py
+++ b/solution.py
@@ -639,15 +639,6 @@
                 res_e[q, i, R] = (rows[R][i] + v + 0.3 * nz[q, i, R].astype(F32)).astype(BF)
         return carry
 
-    lax.fori_loop(0, 4, early_conv, 0)
-    late_copies = reduce_frames(late_copies, s1l, r1l, s2l, r2l, sem_l2)
-    for q in range(1, 8):
-        pair_rows(q, "wait")
-    lax.fori_loop(1, 8, edges(0), 0)
-    side_copies(1, 7, 0, 2, "start")
-    tb_copy = pltpu.make_async_copy(tb, tb_out, osem.at[1])
-    tb_copy.start()
-    lax.fori_loop(4, 8, early_conv, 0)
     for i, (at, nxt) in enumerate(ENDS):
         norm_frame(at, nxt, E_ROWS * i + 3, i, pb, tb, ed, stat_e, gain, bias, ea.at[i], ll_x, None, keeps)
     rows = conv_rows(5, ll_x, w0, w1)
@@ -658,6 +649,15 @@
                 v = v + pb[nxt[0], nxt[1], R]
             v = v.astype(F32) * (1.0 if nxt is None else 0.5)
             res_x[i, R] = (rows[R][i] + v + 0.3 * nz_x[i, R].astype(F32)).astype(BF)
+    lax.fori_loop(0, 4, early_conv, 0)
+    late_copies = reduce_frames(late_copies, s1l, r1l, s2l, r2l, sem_l2)
+    for q in range(1, 8):
+        pair_rows(q, "wait")
+    lax.fori_loop(1, 8, edges(0), 0)
+    side_copies(1, 7, 0, 2, "start")
+    tb_copy = pltpu.make_async_copy(tb, tb_out, osem.at[1])
+    tb_copy.start()
+    lax.fori_loop(4, 8, early_conv, 0)
     early_copy = pltpu.make_async_copy(res_e, early_out, osem.at[3])
     early_copy.start()
     ends_copy = pltpu.make_async_copy(res_x, ends_out, osem.at[5])

time: 79.1 us -> 78.7 us (level)
  no operation moved by 1% of the time
where the time goes in v3:
time: 78.7 us; the launch traced here: 78.6 us
  Pallas kernels  78.4 us (100%)
    pallas_call x1, Pallas kernels, local(): pl.pallas_call(move_kernel, out_shape=(jax.ShapeDtypeStruct((quads, 4, 8,...  68.2 us
    pallas_call x1, Pallas kernels, local(): pl.pallas_call(conv_kernel, out_shape=jax.ShapeDtypeStruct((64, 8, 32, 12...  10.2 us

profile of v3, /device:TPU:1, one launch (start us, length us, event | category | flops | bytes accessed | tf_op | source)
XLA Modules:
  0.0 78.6 jit_solution(13447500978052784952)
XLA Ops:
  0.0 68.2 %move.1 = (bf16[9,4,8,32,128]{4,3,2,1,0:T(8,128)(2,1)}, bf16[2,9,4,32,128]{4,3,2,1,0:T(8,128)(2,1)}, bf16[2,9,4,16,128]{4,3,2,1,0:T(8,128)(2,1)}, f32[2,48,128]{...) custom-call(bf16[2,8,512,256]{3,2,1,0:T(8,128)(2,1)} %video.1, ...), custom_call_target="tpu_custom_call" | custom-call | tf_op jit(solution)/shard_map/move/pallas_call | solution.py:715
  68.2 10.2 %conv.1 = bf16[64,8,32,128]{3,2,1,0:T(8,128)(2,1)} custom-call(bf16[9,4,8,32,128]{4,3,2,1,0:T(8,128)(2,1)} %get-tuple-element.11.pb_in, bf16[2,9,4,32,128]{4,3,2,1,0:T(8,128)(2,1)} %get-tuple-element.12.tb_in, bf16[2,9,4,16,128]{4,3,2,1,0:T(8,128)(2,1)} %get-tuple-element.13.ed_in, f32[2,48,128]{2,1,0:T(8,128)} %get-tuple-element.14.st_in, ...), custom_call_target="tpu_custom_call" | custom-call | tf_op jit(solution)/shard_map/conv/pallas_call | solution.py:780
